TPU v7x, 32 devices: a whole 2x2x4 slice. The times are simulated.
32 devices in a mesh: batch: 4 (over z), head: 2 (over core), seq: 4 (over y, x).
Axes of the slice: x: 2, y: 2, z: 4, core: 2. Of those that a mesh axis runs over, the one named last changes fastest.
Arguments:
- hidden: float32 [8192, 8192], P(('batch', 'seq')), parts along dimension 0, may hold values from -6 to 6
- row_scale: float32 [8192], P(('batch', 'seq')), parts along dimension 0, may hold values from 0.25 to 4
- key_value_weight: float32 [8192, 8, 256], P('seq', 'head'), may hold values from -0.0625 to 0.0625
- outlier: int32 [128, 8], P(('batch', 'seq'), 'head'), parts along dimension 0, may hold values 0 or 1
- sketch_sign_flags: int32 [8, 2, 128, 64], P('head'), may hold values from 0 to 1
Outputs:
- left: bfloat16 [8, 8192, 128], P('head', ('batch', 'seq')), parts along dimension 1
- right: float32 [32, 128, 128], P(('batch', 'head')), parts along dimension 0
There are 4 independent parts, one for each index of `batch`. A program takes and returns all parts, laid end to end along the dimension named above; an argument that names none is the same for every part. Nothing has to cross between parts.
All inputs are finite; a program needn't handle non-finite values. No bound on the sum of `outlier` on one device may be relied on, other than what follows from the above.
Results may differ from a plain program's by a relative error of at most 0.0015.
Values sent between devices are 32-bit elements; how exact they have to be, the bound alone decides.
A program may use at most 192 MiB of HBM per device.

v0:
```python
import math

import jax
import jax.numpy as jnp
from jax import lax
from jax.sharding import PartitionSpec as P

ITERS = 2


complete_cycle = 2.0 * math.pi


def shards(hidden, row_scale, key_value_weight, outlier, sketch_sign_flags):
    tok_rows = hidden.shape[0]
    head_count = key_value_weight.shape[1]
    kv_cols = key_value_weight.shape[2]
    head_dim = kv_cols // 2
    rank_cols = sketch_sign_flags.shape[3]
    group_count = outlier.shape[0]
    highest = lax.Precision.HIGHEST
    weight_piece = lax.all_gather(key_value_weight, "seq", axis=0, tiled=True)
    flat_piece = weight_piece.reshape(weight_piece.shape[0], head_count * kv_cols)
    projected_key_value = jnp.dot(hidden, flat_piece, precision=highest)
    projected_key_value = projected_key_value * row_scale[:, None]
    grouped_rows = projected_key_value.reshape(
        group_count, tok_rows // group_count, head_count, kv_cols
    )
    quantization_spacing = jnp.max(jnp.abs(grouped_rows), axis=1, keepdims=True) / 7.0 + 1e-06
    retain_mask = (1 - outlier).astype(jnp.float32)[:, None, :, None]
    residual_error = (
        retain_mask * jnp.sin(complete_cycle * grouped_rows / quantization_spacing)
    ).reshape(tok_rows, head_count, 2, head_dim)
    sign_matrix = (2 * sketch_sign_flags - 1).astype(jnp.float32)
    sketch = jnp.einsum("thec,heck->thek", residual_error, sign_matrix, precision=highest)
    for iteration in range(ITERS):
        local_gram = jnp.einsum("thek,theq->hekq", sketch, sketch, precision=highest)
        gram_matrix = lax.psum(local_gram, "seq")
        lower_factor = jnp.linalg.cholesky(gram_matrix)
        identity = jnp.broadcast_to(jnp.eye(rank_cols, dtype=gram_matrix.dtype), gram_matrix.shape)
        inverse_factor = jax.scipy.linalg.solve_triangular(lower_factor, identity, lower=True)
        basis_matrix = jnp.einsum("thek,heqk->theq", sketch, inverse_factor, precision=highest)
        local_coef = jnp.einsum("thec,theq->hecq", residual_error, basis_matrix, precision=highest)
        coefficient_rows = lax.psum(local_coef, "seq")
        if iteration + 1 < ITERS:
            sketch = jnp.einsum(
                "thec,hecq->theq", residual_error, coefficient_rows, precision=highest
            )
    root_length = math.sqrt(tok_rows * lax.axis_size("seq"))
    left = (
        (root_length * basis_matrix)
        .transpose(1, 0, 2, 3)
        .reshape(head_count, tok_rows, 2 * rank_cols)
        .astype(jnp.bfloat16)
    )
    right = (
        (coefficient_rows / root_length)
        .transpose(0, 2, 1, 3)
        .reshape(head_count, head_dim, 2 * rank_cols)
    )
    return (left, right)


def solution(mesh):
    return jax.shard_map(
        shards,
        mesh=mesh,
        in_specs=(
            P(("batch", "seq"), None),
            P(("batch", "seq")),
            P("seq", "head", None),
            P(("batch", "seq"), "head"),
            P("head", None, None, None),
        ),
        out_specs=(P("head", ("batch", "seq"), None), P(("batch", "head"), None, None)),
        check_vma=False,
    )
```

profile of v0, /device:TPU:0, one launch (start us, length us, event | category | flops | bytes accessed | tf_op | source)
XLA Modules:
  0.0 796.7 jit_solution(14523323449922027242)
XLA Ops:
  7.2 0.0 copy-start.2
  7.2 0.0 all-gather.2.cloned.1.call-start
  7.2 0.7 all-gather.2.cloned.1.call-update
  7.9 0.0 all-reduce.5.cloned.1.call-start
  8.0 0.0 copy-done.2
  8.0 0.1 mul.45
  8.0 0.1 mul.46
  8.1 301.7 %all-gather.2.cloned.1.call-done = f32[8192,4,256]{2,1,0:T(4,128)} async-done(((f32[2048,4,256]{2,1,0:T(4,128)}), f32[8192,4,256]{2,1,0:T(4,128)}) %all-gather.2.cloned.1.call-update) | async-done | bytes 33554448 | tf_op jit(solution)/shard_map/all_gather | solution.py:22
  309.8 0.0 copy-start.3
  309.8 27.5 %copy.108 = f32[1024,8,4,256]{3,1,2,0:T(8,128)} copy(f32[1024,8,4,256]{3,2,1,0:T(4,128)} %bitcast.58) | data formatting | bytes 67108864
  337.3 0.0 copy-done.3
  337.3 60.5 %multiply_abs_fusion = (f32[512,1024]{1,0:T(8,128)}, f32[512,1024]{1,0:T(8,128)}) fusion(f32[512]{0:T(512)S(1)} %copy-done.3, f32[512,8192]{1,0:T(8,128)} %param.8, f32[8192,1024]{1,0:T(8,128)} %bitcast.59), kind=kOutput, calls=%fused_computation.3 | convolution fusion | flops 51541180416 | bytes 54528000 | tf_op jit(solution)/shard_map/dot_general | solution.py:24
  397.8 2.2 abs.7
  400.0 0.3 reduce_max.9
  400.3 0.2 div.31
  400.5 2.1 div.32
  402.7 1.9 copy.86
  404.6 1.8 copy.88
  406.4 0.0 copy-start.1
  406.4 8.9 %fusion.1 = f32[512,4,2,128]{3,0,2,1:T(8,128)S(1)} fusion(f32[512,4,2,128]{3,0,2,1:T(8,128)} %copy.88, f32[512,4,2,128]{3,2,0,1:T(2,128)} %div.32, f32[512,4]{0,1:T(4,128)S(1)} %mul.46), kind=kLoop, calls=%fused_computation.2 | loop fusion | flops 1048576 | bytes 6299648 | tf_op jit(solution)/shard_map/mul | solution.py:32
  415.3 0.0 copy-done.1
  415.3 2.4 convolution_bitcast_fusion.1
  417.7 1.8 fusion.21
  419.5 0.0 all-reduce.5.cloned.1.call-update
  419.5 0.0 all-reduce.7.cloned.1.call-start
  419.6 43.0 %all-reduce.5.cloned.1.call-done = f32[4,2,64,64]{2,3,1,0:T(8,128)} async-done(((f32[4,2,64,64]{2,3,1,0:T(8,128)}), f32[4,2,64,64]{2,3,1,0:T(8,128)}) %all-reduce.5.cloned.1.call-update) | async-done | bytes 131088 | tf_op jit(solution)/shard_map/psum | solution.py:38
  462.6 1.1 copy.91
  463.7 1.7 fusion.9
  465.4 47.6 %custom-call.8 = f32[4,2,64,64]{3,2,1,0:T(8,128)S(1)} custom-call(f32[4,2,64,64]{3,2,1,0:T(8,128)} %fusion.9), custom_call_target="Cholesky" | custom-call | tf_op jit(solution)/shard_map/jit(cholesky)/cholesky | solution.py:39
  513.0 0.1 compare_reduce_fusion.1
  513.2 0.8 select_bitcast_fusion.1
  514.0 40.0 %custom-call.9 = f32[4,2,1,64,64]{3,4,2,1,0:T(8,128)S(1)} custom-call(f32[4,2,1,64,64]{4,3,2,1,0:T(8,128)} %select_bitcast_fusion.1), custom_call_target="InvertDiagBlocksLowerTriangular" | custom-call | tf_op jit(solution)/shard_map/jit(_solve_triangular)/vmap(vmap())/triangular_solve | solution.py:41
  554.1 0.6 fusion.7
  554.7 1.0 convolution_bitcast_fusion.2
  555.6 2.2 fusion.22
  557.9 0.0 all-reduce.7.cloned.1.call-update
  557.9 0.0 all-reduce.9.cloned.1.call-start
  558.0 43.0 %all-reduce.7.cloned.1.call-done = f32[4,2,128,64]{2,3,1,0:T(8,128)} async-done(((f32[4,2,128,64]{2,3,1,0:T(8,128)}), f32[4,2,128,64]{2,3,1,0:T(8,128)}) %all-reduce.7.cloned.1.call-update) | async-done | bytes 262160 | tf_op jit(solution)/shard_map/psum | solution.py:44
  601.0 3.3 convolution_bitcast_fusion
  604.3 1.8 fusion.23
  606.1 0.0 all-reduce.9.cloned.1.call-update
  606.1 0.0 all-reduce.11.cloned.1.call-start
  606.1 43.0 %all-reduce.9.cloned.1.call-done = f32[4,2,64,64]{2,3,1,0:T(8,128)} async-done(((f32[4,2,64,64]{2,3,1,0:T(8,128)}), f32[4,2,64,64]{2,3,1,0:T(8,128)}) %all-reduce.9.cloned.1.call-update) | async-done | bytes 131088 | tf_op jit(solution)/shard_map/psum | solution.py:38
  649.2 1.1 copy.96
  650.3 1.7 fusion.6
  652.0 47.6 %custom-call.10 = f32[4,2,64,64]{3,2,1,0:T(8,128)S(1)} custom-call(f32[4,2,64,64]{3,2,1,0:T(8,128)} %fusion.6), custom_call_target="Cholesky" | custom-call | tf_op jit(solution)/shard_map/jit(cholesky)/cholesky | solution.py:39
  699.6 0.1 compare_reduce_fusion
  699.8 0.8 select_bitcast_fusion
  700.6 40.0 %custom-call.11 = f32[4,2,1,64,64]{3,4,2,1,0:T(8,128)S(1)} custom-call(f32[4,2,1,64,64]{4,3,2,1,0:T(8,128)} %select_bitcast_fusion), custom_call_target="InvertDiagBlocksLowerTriangular" | custom-call | tf_op jit(solution)/shard_map/jit(_solve_triangular)/vmap(vmap())/triangular_solve | solution.py:41
  740.6 0.6 fusion.4
  741.2 1.8 multiply_convert_fusion
  743.0 0.0 copy-start
  743.0 2.2 fusion.2
  745.3 0.0 all-reduce.11.cloned.1.call-update
  745.3 0.0 copy-done
  745.3 1.0 copy.100
  746.3 42.1 %all-reduce.11.cloned.1.call-done = f32[4,2,128,64]{2,3,1,0:T(8,128)} async-done(((f32[4,2,128,64]{2,3,1,0:T(8,128)}), f32[4,2,128,64]{2,3,1,0:T(8,128)}) %all-reduce.11.cloned.1.call-update) | async-done | bytes 262160 | tf_op jit(solution)/shard_map/psum | solution.py:44
  788.4 1.0 broadcast_multiply_fusion
  789.3 0.8 copy.101
  (7 shorter events, 0.1 us)
Async XLA Ops:
  7.2 0.8 copy-start.2
  7.2 302.6 %all-gather.2.cloned.1.call-start = ((), (), s32[]{:S(2)}) async-start(), calls=%async_computation | async-start | bytes 41943040 | tf_op jit(solution)/shard_map/all_gather | solution.py:22
  7.9 454.7 %all-reduce.5.cloned.1.call-start = ((), (), s32[]{:S(2)}) async-start(), calls=%async_computation.1 | async-start | bytes 524288 | tf_op jit(solution)/shard_map/psum | solution.py:38
  309.8 27.5 %copy-start.3 = (f32[512]{0:T(512)S(1)}, f32[512]{0:T(512)}, u32[]{:S(2)}) copy-start(f32[512]{0:T(512)} %param.9) | copy-start | bytes 6148
  406.4 8.9 %copy-start.1 = (s32[4,2,128,64]{2,3,1,0:T(8,128)S(1)}, s32[4,2,128,64]{2,3,1,0:T(8,128)}, u32[]{:S(2)}) copy-start(s32[4,2,128,64]{2,3,1,0:T(8,128)} %param.12) | copy-start | bytes 786436
  419.5 181.5 %all-reduce.7.cloned.1.call-start = ((), (), s32[]{:S(2)}) async-start(), calls=%async_computation.2 | async-start | bytes 524288 | tf_op jit(solution)/shard_map/psum | solution.py:44
  557.9 91.3 %all-reduce.9.cloned.1.call-start = ((), (), s32[]{:S(2)}) async-start(), calls=%async_computation.3 | async-start | bytes 524288 | tf_op jit(solution)/shard_map/psum | solution.py:38
  606.1 182.3 %all-reduce.11.cloned.1.call-start = ((), (), s32[]{:S(2)}) async-start(), calls=%async_computation.4 | async-start | bytes 524288 | tf_op jit(solution)/shard_map/psum | solution.py:44
  743.0 2.3 copy-start
Sparse Core Ops, SparseCore 0:
  9.8 299.9 all-gather.1
  419.6 42.9 all-reduce.4
  558.0 42.9 all-reduce.6
  606.2 42.9 all-reduce.8
  745.4 42.9 all-reduce.10
where the time goes:
time: 798 us; the launch traced here: 797 us
  waiting for transfers between devices  474 us (59%)
  other arithmetic  191 us (24%)
  matrix products  78.2 us (10%)
  local copies, waits for them, and re-layouts  39.9 us (5%)
  between operations  14 us (2%)
    all_gather x1, waiting for transfers between devices, shards(): weight_piece = lax.all_gather(key_value_weight, 'seq', axis=0, tiled=True)  302 us
    another operation x7, other arithmetic, shards(): lower_factor = jnp.linalg.cholesky(gram_matrix)  95.6 us
    psum x2, waiting for transfers between devices, shards(): gram_matrix = lax.psum(local_gram, 'seq')  86 us
    psum x2, waiting for transfers between devices, shards(): coefficient_rows = lax.psum(local_coef, 'seq')  85.1 us
    another operation x5, other arithmetic, shards(): jax.scipy.linalg.solve_triangular(lower_factor, identity, lower=True)  81.7 us
    dot_general x1, matrix products, shards(): projected_key_value = jnp.dot(hidden, flat_piece, precision=highest)  60.5 us
    unnamed x11, local copies, waits for them, and re-layouts  29.4 us
  transfers between devices with their start and end apart: 5, of which 5 were waited for; matrix products, arithmetic and copies ran while one was open for 0% of the time, Pallas kernels for 0%

commit v1 on v0

--- a/solution.py
+++ b/solution.py
@@ -1,14 +1,392 @@
+import functools
 import math
 
 import jax
 import jax.numpy as jnp
+import numpy as np
 from jax import lax
+from jax.experimental import pallas as pl
+from jax.experimental.pallas import tpu as pltpu
 from jax.sharding import PartitionSpec as P
 
 ITERS = 2
-
+MESH = pl.DeviceIdType.MESH
+HIGHEST = lax.Precision.HIGHEST
 
 complete_cycle = 2.0 * math.pi
+
+
+def sine_coefficients(terms=8):
+    nodes = np.cos(np.pi * (np.arange(400) + 0.5) / 400)
+    r = 0.25 + 0.25 * nodes
+    values = np.sin(2 * np.pi * r) / r
+    square = r * r
+    scaled = square * 8 - 1
+    fit = np.polynomial.chebyshev.chebfit(scaled, values, terms - 1)
+    series = np.polynomial.chebyshev.cheb2poly(fit)
+    power = np.zeros(1)
+    for c in series[::-1]:
+        power = np.polynomial.polynomial.polyadd(
+            np.polynomial.polynomial.polymul(power, [-1.0, 8.0]), [c]
+        )
+    return [float(c) for c in power[:terms]]
+
+
+SINE = sine_coefficients()
+
+
+def sine_of_cycles(x):
+    r = x - jnp.round(x)
+    s = r * r
+    total = jnp.full_like(s, SINE[-1])
+    for c in SINE[-2::-1]:
+        total = total * s + c
+    return total * r
+
+
+def split(x):
+    hi = x.astype(jnp.bfloat16)
+    return hi, (x - hi.astype(jnp.float32)).astype(jnp.bfloat16)
+
+
+def dot(a, b):
+    return jnp.dot(a, b, preferred_element_type=jnp.float32)
+
+
+def dot_nt(a, b, precision=None):
+    return lax.dot_general(
+        a, b, (((1,), (1,)), ((), ())), precision=precision, preferred_element_type=jnp.float32
+    )
+
+
+def inverse_factors(grams):
+    k = grams[0].shape[0]
+    sub = lax.broadcasted_iota(jnp.int32, (k, 2 * k), 0)
+    lane = lax.broadcasted_iota(jnp.int32, (k, 2 * k), 1)
+    start = []
+    for gram in grams:
+        eye = (sub[:, :k] == lane[:, :k]).astype(jnp.float32)
+        start.append(jnp.concatenate([gram, eye], axis=1))
+
+    def step(i, state):
+        out = []
+        for x in state:
+            row = jnp.sum(jnp.where(sub == i, x, 0.0), axis=0, keepdims=True)
+            column = jnp.sum(jnp.where(lane == i, x, 0.0), axis=1, keepdims=True)
+            pivot = jnp.sum(jnp.where(lane[:1] == i, row, 0.0), axis=1, keepdims=True)
+            factor = jnp.where(sub[:, :1] > i, column / pivot, 0.0)
+            out.append(x - factor * row)
+        return tuple(out)
+
+    done = lax.fori_loop(0, k, step, tuple(start))
+    result = []
+    for x in done:
+        pivots = jnp.sum(jnp.where(sub == lane, x, 0.0), axis=1, keepdims=True)
+        result.append(x[:, k:] * lax.rsqrt(pivots))
+    return result
+
+
+def kernel(
+    n, groups, root, hid, whi_h, wlo_h, scale, retain, signs, left, right,
+    whi, wlo, own, got, part, sums, res, gsend, grecv, factors, frecv,
+    wsem, osem, hsend, hrecv, fsend, frsem, psend, precv, gs, gr, ms, mr,
+):
+    me = lax.axis_index("seq")
+    core = lax.axis_index("head")
+    tok, kblk = own.shape
+    cols = whi.shape[1]
+    half = tok // 2
+    pieces = 2
+    chunk = half // pieces
+    heads = cols // 256
+
+    def peer(r):
+        return lax.rem(me + r, n)
+
+    barrier = pltpu.get_barrier_semaphore()
+    for r in range(1, n):
+        pl.semaphore_signal(barrier, inc=1, device_id={"seq": peer(r)}, device_id_type=MESH)
+    pl.semaphore_signal(barrier, inc=1, device_id={"head": 1 - core}, device_id_type=MESH)
+
+    load_own = pltpu.make_async_copy(
+        hid.at[:, pl.ds(pl.multiple_of(me * kblk, 128), kblk)], own, osem
+    )
+    load_own.start()
+    load_hi = pltpu.make_async_copy(whi_h, whi, wsem.at[0])
+    load_lo = pltpu.make_async_copy(wlo_h, wlo, wsem.at[1])
+    load_hi.start()
+    load_lo.start()
+    pl.semaphore_wait(barrier, n)
+
+    def rows_of(which, q):
+        return pl.ds(pl.multiple_of(which * half + q * chunk, chunk), chunk)
+
+    def hidden_copy(q, r):
+        p = lax.rem(me + r, n)
+        return pltpu.make_async_remote_copy(
+            src_ref=hid.at[rows_of(core, q), pl.ds(pl.multiple_of(p * kblk, 128), kblk)],
+            dst_ref=got.at[n - r - 1, rows_of(core, q)],
+            send_sem=hsend.at[q, r - 1],
+            recv_sem=hrecv.at[q, n - r - 1],
+            device_id={"seq": p},
+            device_id_type=MESH,
+        )
+
+    def hidden_arrival(q, slot):
+        return pltpu.make_async_remote_copy(
+            src_ref=got.at[slot, rows_of(core, q)],
+            dst_ref=got.at[slot, rows_of(core, q)],
+            send_sem=hsend.at[q, slot],
+            recv_sem=hrecv.at[q, slot],
+            device_id={"seq": lax.rem(me + slot + 1, n)},
+            device_id_type=MESH,
+        )
+
+    def forward_copy(q, slot, which):
+        return pltpu.make_async_remote_copy(
+            src_ref=got.at[slot, rows_of(which, q)],
+            dst_ref=got.at[slot, rows_of(which, q)],
+            send_sem=fsend.at[q, slot],
+            recv_sem=frsem.at[q, slot],
+            device_id={"head": 1 - core},
+            device_id_type=MESH,
+        )
+
+    def part_copy(slot, which, q):
+        r = slot + 1
+        return pltpu.make_async_remote_copy(
+            src_ref=part.at[slot, rows_of(which, q)],
+            dst_ref=sums.at[n - r - 1, rows_of(which, q)],
+            send_sem=psend.at[slot, which, q],
+            recv_sem=precv.at[n - r - 1, which, q],
+            device_id={"seq": lax.rem(me + r, n)},
+            device_id_type=MESH,
+        )
+
+    def part_arrival(slot, which, q):
+        return pltpu.make_async_remote_copy(
+            src_ref=sums.at[slot, rows_of(which, q)],
+            dst_ref=sums.at[slot, rows_of(which, q)],
+            send_sem=psend.at[slot, which, q],
+            recv_sem=precv.at[slot, which, q],
+            device_id={"seq": lax.rem(me + slot + 1, n)},
+            device_id_type=MESH,
+        )
+
+    for q in range(pieces):
+        for r in range(1, n):
+            hidden_copy(q, r).start()
+
+    def project(src, dst, rows):
+        hi, lo = split(src[rows])
+
+        def tile(t, carry):
+            c = pl.ds(pl.multiple_of(t * 256, 256), 256)
+            w = whi[:, c]
+            dst[rows, c] = dot(hi, w) + dot(lo, w) + dot(hi, wlo[:, c])
+            return carry
+
+        lax.fori_loop(0, cols // 256, tile, 0)
+
+    load_own.wait()
+    load_hi.wait()
+    load_lo.wait()
+
+    def own_step(i, carry):
+        project(own, res, pl.ds(pl.multiple_of(i * chunk, chunk), chunk))
+        return carry
+
+    lax.fori_loop(0, tok // chunk, own_step, 0)
+
+    def step(i, carry):
+        q = i // (n - 1)
+        slot = lax.rem(i, n - 1)
+        hidden_arrival(q, slot).wait_recv()
+        forward_copy(q, slot, core).start()
+
+        def side(j, carry):
+            which = lax.rem(core + j, 2)
+
+            @pl.when(j == 1)
+            def _():
+                forward_copy(q, slot, which).wait_recv()
+
+            project(got.at[slot], part.at[slot], rows_of(which, q))
+            part_copy(slot, which, q).start()
+            return carry
+
+        lax.fori_loop(0, 2, side, 0)
+        return carry
+
+    lax.fori_loop(0, pieces * (n - 1), step, 0)
+
+    group = tok // groups
+    per = chunk // group
+
+    def residual(i, carry):
+        which = i // pieces
+        q = lax.rem(i, pieces)
+        for slot in range(n - 1):
+            part_arrival(slot, which, q).wait_recv()
+        for g in range(per):
+            at = i * per + g
+            rows = pl.ds(pl.multiple_of(at * group, group), group)
+            kv = res[rows]
+            for slot in range(n - 1):
+                kv = kv + sums[slot, rows]
+            kv = kv * scale[rows]
+            spacing = jnp.max(jnp.abs(kv), axis=0, keepdims=True) / 7.0 + 1e-06
+            res[rows] = retain[pl.ds(at, 1)] * sine_of_cycles(kv * (1.0 / spacing))
+        return carry
+
+    lax.fori_loop(0, 2 * pieces, residual, 0)
+
+    def square(h, carry):
+        for e in range(2):
+            hi, lo = split(res[:, pl.ds(pl.multiple_of(h * 256 + e * 128, 128), 128)])
+            both = jnp.concatenate([hi, lo], axis=1)
+            g = lax.dot_general(
+                both, both, (((0,), (0,)), ((), ())), preferred_element_type=jnp.float32
+            )
+            gsend[h, e] = g[:128, :128] + (g[:128, 128:] + g[128:, :128])
+        return carry
+
+    lax.fori_loop(0, heads, square, 0)
+
+    def gram_copy(r):
+        p = peer(r)
+        return pltpu.make_async_remote_copy(
+            src_ref=gsend.at[p],
+            dst_ref=grecv.at[n - r - 1],
+            send_sem=gs.at[r - 1],
+            recv_sem=gr.at[n - r - 1],
+            device_id={"seq": p},
+            device_id_type=MESH,
+        )
+
+    for r in range(1, n):
+        gram_copy(r).start()
+    for r in range(1, n):
+        gram_copy(r).wait_recv()
+
+    total = [gsend[me, e] for e in range(2)]
+    for slot in range(n - 1):
+        total = [total[e] + grecv[slot, e] for e in range(2)]
+    sketch = [signs[me, e] for e in range(2)]
+    for iteration in range(ITERS):
+        product = [jnp.dot(sketch[e], total[e], precision=HIGHEST) for e in range(2)]
+        inverse = inverse_factors([dot_nt(product[e], sketch[e], HIGHEST) for e in range(2)])
+        coefficient = [jnp.dot(inverse[e], product[e], precision=HIGHEST) for e in range(2)]
+        if iteration + 1 < ITERS:
+            sketch = coefficient
+        else:
+            sketch = [jnp.dot(inverse[e], sketch[e], precision=HIGHEST) for e in range(2)]
+    rank = sketch[0].shape[0]
+    for e in range(2):
+        factors[0, e * rank : (e + 1) * rank] = sketch[e] * root
+    factors[1] = jnp.concatenate(coefficient, axis=0).T * (1.0 / root)
+
+    def factor_copy(r):
+        return pltpu.make_async_remote_copy(
+            src_ref=factors,
+            dst_ref=frecv.at[n - r - 1],
+            send_sem=ms.at[r - 1],
+            recv_sem=mr.at[n - r - 1],
+            device_id={"seq": peer(r)},
+            device_id_type=MESH,
+        )
+
+    for r in range(1, n):
+        factor_copy(r).start()
+
+    def finish(h, matrix, coefficient_rows):
+        zero = jnp.zeros((rank, 128), jnp.float32)
+        block = jnp.concatenate(
+            [
+                jnp.concatenate([matrix[:rank], zero], axis=1),
+                jnp.concatenate([zero, matrix[rank:]], axis=1),
+            ],
+            axis=0,
+        )
+        mhi, mlo = split(block)
+        hi, lo = split(res[:, pl.ds(pl.multiple_of(h * 256, 256), 256)])
+        value = dot_nt(hi, mhi) + (dot_nt(lo, mhi) + dot_nt(hi, mlo))
+        left[h] = value.astype(jnp.bfloat16)
+        right[h] = coefficient_rows
+
+    finish(me, factors[0], factors[1])
+    for r in range(1, n):
+        slot = r - 1
+        factor_copy(n - r).wait_recv()
+        finish(peer(r), frecv[slot, 0], frecv[slot, 1])
+
+    for q in range(pieces):
+        for r in range(1, n):
+            hidden_copy(q, r).wait_send()
+            forward_copy(q, r - 1, core).wait_send()
+            for which in range(2):
+                part_copy(r - 1, which, q).wait_send()
+    for r in range(1, n):
+        gram_copy(r).wait_send()
+        factor_copy(r).wait_send()
+
+
+def fast_shards(n, hidden, row_scale, key_value_weight, outlier, sketch_sign_flags):
+    tok = hidden.shape[0]
+    kblk, heads, per_head = key_value_weight.shape
+    cols = heads * per_head
+    groups = outlier.shape[0]
+    flat = key_value_weight.reshape(kblk, cols)
+    top = lax.reduce_precision(flat, exponent_bits=8, mantissa_bits=7)
+    whi = top.astype(jnp.bfloat16)
+    wlo = (flat - top).astype(jnp.bfloat16)
+    retain = jnp.repeat((1 - outlier).astype(jnp.float32), per_head, axis=1)
+    signs = (2 * sketch_sign_flags - 1).astype(jnp.float32).transpose(0, 1, 3, 2)
+    f32 = jnp.float32
+    any_spec = pl.BlockSpec(memory_space=pl.ANY)
+    vmem = pl.BlockSpec(memory_space=pltpu.VMEM)
+    dma = pltpu.SemaphoreType.DMA
+    left, right = pl.pallas_call(
+        functools.partial(kernel, n, groups, math.sqrt(tok * n)),
+        out_shape=(
+            jax.ShapeDtypeStruct((heads, tok, 128), jnp.bfloat16),
+            jax.ShapeDtypeStruct((heads, 128, 128), f32),
+        ),
+        in_specs=[any_spec, any_spec, any_spec, vmem, vmem, vmem],
+        out_specs=(vmem, vmem),
+        scratch_shapes=[
+            pltpu.VMEM((kblk, cols), jnp.bfloat16),
+            pltpu.VMEM((kblk, cols), jnp.bfloat16),
+            pltpu.VMEM((tok, kblk), f32),
+            pltpu.VMEM((n - 1, tok, kblk), f32),
+            pltpu.VMEM((n - 1, tok, cols), f32),
+            pltpu.VMEM((n - 1, tok, cols), f32),
+            pltpu.VMEM((tok, cols), f32),
+            pltpu.VMEM((heads, 2, 128, 128), f32),
+            pltpu.VMEM((n - 1, 2, 128, 128), f32),
+            pltpu.VMEM((2, 128, 128), f32),
+            pltpu.VMEM((n - 1, 2, 128, 128), f32),
+            dma((2,)),
+            dma,
+            dma((2, n - 1)),
+            dma((2, n - 1)),
+            dma((2, n - 1)),
+            dma((2, n - 1)),
+            dma((n - 1, 2, 2)),
+            dma((n - 1, 2, 2)),
+            dma((n - 1,)),
+            dma((n - 1,)),
+            dma((n - 1,)),
+            dma((n - 1,)),
+        ],
+        compiler_params=pltpu.CompilerParams(
+            collective_id=0, has_side_effects=True, vmem_limit_bytes=56 * 1024 * 1024
+        ),
+        cost_estimate=pl.CostEstimate(
+            flops=6 * n * tok * kblk * cols, bytes_accessed=4 * n * tok * kblk, transcendentals=0
+        ),
+    )(hidden, whi, wlo, row_scale[:, None], retain, signs)
+    return left, right
 
 
 def shards(hidden, row_scale, key_value_weight, outlier, sketch_sign_flags):
@@ -62,16 +440,26 @@
 
 
 def solution(mesh):
-    return jax.shard_map(
-        shards,
-        mesh=mesh,
-        in_specs=(
-            P(("batch", "seq"), None),
-            P(("batch", "seq")),
-            P("seq", "head", None),
-            P(("batch", "seq"), "head"),
-            P("head", None, None, None),
-        ),
-        out_specs=(P("head", ("batch", "seq"), None), P(("batch", "head"), None, None)),
-        check_vma=False,
-    )
+    def run(hidden, row_scale, key_value_weight, outlier, sketch_sign_flags):
+        members = mesh.shape["seq"]
+        heads = key_value_weight.shape[1] // mesh.shape["head"]
+        fits = members == 4 and heads == members and mesh.shape["head"] == 2
+        chosen = functools.partial(fast_shards, members) if fits else shards
+        return mapped(chosen)(hidden, row_scale, key_value_weight, outlier, sketch_sign_flags)
+
+    def mapped(chosen):
+        return jax.shard_map(
+            chosen,
+            mesh=mesh,
+            in_specs=(
+                P(("batch", "seq"), None),
+                P(("batch", "seq")),
+                P("seq", "head", None),
+                P(("batch", "seq"), "head"),
+                P("head", None, None, None),
+            ),
+            out_specs=(P("head", ("batch", "seq"), None), P(("batch", "head"), None, None)),
+            check_vma=False,
+        )
+
+    return run

time: 798 us -> 241 us (0.30)
  waiting for transfers between devices: 474 us -> 0 us
  Pallas kernels: 0 us -> 223 us
  other arithmetic: 191 us -> 5.84 us
  matrix products: 78.2 us -> 0 us
  local copies, waits for them, and re-layouts: 39.9 us -> 10.6 us
  between operations: 14 us -> 0.67 us
    all_gather x1 -> x0, waiting for transfers between devices: 302 us -> none  [shards(): weight_piece = lax.all_gather(key_value_weight, 'seq', axis=0, tiled=True)]
    pallas_call x0 -> x1, Pallas kernels: none -> 223 us  [fast_shards(): pl.pallas_call(functools.partial(kernel, n, groups, math.sqrt(tok * n)),...]
    another operation x12 -> x0, other arithmetic: 177 us -> none  [the longest x7 95.6 us: shards(): lower_factor = jnp.linalg.cholesky(gram_matrix)]
    psum x4 -> x0, waiting for transfers between devices: 171 us -> none  [the longest x2 86 us: shards(): gram_matrix = lax.psum(local_gram, 'seq')]
    dot_general x9 -> x0, matrix products: 77 us -> none  [the longest x1 60.5 us: shards(): projected_key_value = jnp.dot(hidden, flat_piece, precision=highest)]
    unnamed x11 -> x9, local copies, waits for them, and re-layouts: 29.4 us -> 9.02 us
    mul x1 -> x0, other arithmetic: 8.89 us -> none  [shards(): retain_mask * jnp.sin(complete_cycle * grouped_rows / quantization_spacing)]
  transfers between devices with their start and end apart: 5 -> 0, of which waited for: 5 -> 0; matrix products, arithmetic and copies ran while one was open for 0% -> 0% of each run, Pallas kernels for 0% -> 0%
where the time goes in v1:
time: 241 us
  Pallas kernels  223 us (93%)
  local copies, waits for them, and re-layouts  10.6 us (4%)
  other arithmetic  5.84 us (2%)
    pallas_call x1, Pallas kernels, fast_shards(): pl.pallas_call(functools.partial(kernel, n, groups, math.sqrt(tok * n)),...  223 us
    unnamed x9, local copies, waits for them, and re-layouts  9.02 us
    convert_element_type x1, other arithmetic, fast_shards(): wlo = (flat - top).astype(jnp.bfloat16)  5.11 us

profile of v1, /device:TPU:0, one launch (start us, length us, event | category | flops | bytes accessed | tf_op | source)
XLA Modules:
  0.0 240.5 jit_solution(12314277263807750887)
XLA Ops:
  0.6 5.5 %copy.8 = f32[256,8,4,256]{3,1,2,0:T(8,128)S(1)} copy(f32[256,8,4,256]{3,2,1,0:T(4,128)} %bitcast.7) | data formatting | bytes 16777216
  6.1 0.0 copy-start
  6.1 0.0 copy-start.1
  6.1 0.0 copy-start.2
  6.1 5.1 %fusion = (bf16[2048,1024]{1,0:T(8,128)(2,1)}, bf16[2048,1024]{1,0:T(8,128)(2,1)}) fusion(f32[2048,1024]{1,0:T(8,128)S(1)} %bitcast.6), kind=kLoop, calls=%fused_computation.2 | loop fusion | flops 8388608 | bytes 16777216 | tf_op jit(solution)/shard_map/convert_element_type | solution.py:342
  11.2 0.0 copy-done
  11.2 0.7 convert_bitcast_fusion.signs
  12.0 0.0 copy-done.1
  12.0 0.9 copy.7.scale
  12.8 0.0 copy-done.2
  12.8 0.7 broadcast_in_dim.7
  13.5 223.4 %shard_map.68 = (bf16[4,512,128]{2,1,0:T(8,128)(2,1)}, f32[4,128,128]{2,1,0:T(8,128)}) custom-call(f32[512,8192]{1,0:T(8,128)} %hid.1, bf16[2048,1024]{1,0:T(8,128)(2,1)} %get-tuple-element.3.whi_h, bf16[2048,1024]{1,0:T(8,128)(2,1)} %get-tuple-element.2.wlo_h, f32[512,1]{1,0:T(8,128)} %copy.7.scale, f32[8,1024]{1,0:T(8,128)} %bitcast.8, ...), custom_call_target="tpu_custom_call" | custom-call | flops 25769803776 | bytes 16777216 | tf_op jit(solution)/shard_map/pallas_call | solution.py:349
  237.0 1.9 copy.11
  238.8 1.7 copy.12
  (1 shorter events, 0.0 us)
Async XLA Ops:
  6.1 5.1 %copy-start = (s32[4,2,128,64]{2,3,1,0:T(8,128)S(1)}, s32[4,2,128,64]{2,3,1,0:T(8,128)}, u32[]{:S(2)}) copy-start(s32[4,2,128,64]{2,3,1,0:T(8,128)} %param.9) | copy-start | bytes 786436
  6.1 5.9 %copy-start.1 = (f32[512]{0:T(512)S(1)}, f32[512]{0:T(512)}, u32[]{:S(2)}) copy-start(f32[512]{0:T(512)} %param.6) | copy-start | bytes 6148
  6.1 6.7 %copy-start.2 = (s32[8,4]{0,1:T(4,128)S(1)}, s32[8,4]{0,1:T(4,128)}, u32[]{:S(2)}) copy-start(s32[8,4]{0,1:T(4,128)} %param.8) | copy-start | bytes 388

commit v2 on v1

--- a/solution.py
+++ b/solution.py
@@ -10,6 +10,7 @@
 from jax.sharding import PartitionSpec as P
 
 ITERS = 2
+BLOCK = 4
 MESH = pl.DeviceIdType.MESH
 HIGHEST = lax.Precision.HIGHEST
 
@@ -69,16 +70,29 @@
         start.append(jnp.concatenate([gram, eye], axis=1))
 
     def step(i, state):
+        at = i * BLOCK
         out = []
         for x in state:
-            row = jnp.sum(jnp.where(sub == i, x, 0.0), axis=0, keepdims=True)
-            column = jnp.sum(jnp.where(lane == i, x, 0.0), axis=1, keepdims=True)
-            pivot = jnp.sum(jnp.where(lane[:1] == i, row, 0.0), axis=1, keepdims=True)
-            factor = jnp.where(sub[:, :1] > i, column / pivot, 0.0)
-            out.append(x - factor * row)
+            rows, columns = [], []
+            for t in range(BLOCK):
+                rows.append(jnp.sum(jnp.where(sub == at + t, x, 0.0), axis=0, keepdims=True))
+                picked = jnp.sum(jnp.where(lane == at + t, x, 0.0), axis=1, keepdims=True)
+                columns.append(jnp.broadcast_to(picked, x.shape))
+            for t in range(BLOCK):
+                entry = [
+                    jnp.sum(jnp.where(sub == at + u, columns[t], 0.0), axis=0, keepdims=True)
+                    for u in range(t, BLOCK)
+                ]
+                inverse = 1.0 / entry[0]
+                factor = jnp.where(sub > at + t, columns[t] * inverse, 0.0)
+                for u in range(t + 1, BLOCK):
+                    columns[u] = columns[u] - factor * entry[u - t]
+                    rows[u] = rows[u] - (entry[u - t] * inverse) * rows[t]
+                x = x - factor * rows[t]
+            out.append(x)
         return tuple(out)
 
-    done = lax.fori_loop(0, k, step, tuple(start))
+    done = lax.fori_loop(0, k // BLOCK, step, tuple(start))
     result = []
     for x in done:
         pivots = jnp.sum(jnp.where(sub == lane, x, 0.0), axis=1, keepdims=True)
@@ -87,8 +101,8 @@
 
 
 def kernel(
-    n, groups, root, hid, whi_h, wlo_h, scale, retain, signs, left, right,
-    whi, wlo, own, got, part, sums, res, gsend, grecv, factors, frecv,
+    n, groups, root, hid, weight, scale, retain, signs, left, right,
+    whi, wlo, stage, own, got, part, sums, res, gsend, grecv, factors, frecv,
     wsem, osem, hsend, hrecv, fsend, frsem, psend, precv, gs, gr, ms, mr,
 ):
     me = lax.axis_index("seq")
@@ -100,8 +114,10 @@
     chunk = half // pieces
     heads = cols // 256
 
-    def peer(r):
-        return lax.rem(me + r, n)
+    across = {1: me + 1 - 2 * lax.rem(me, 2), 2: lax.rem(me + 2, n), 3: n - 1 - me}
+
+    def peer(m):
+        return across[m]
 
     barrier = pltpu.get_barrier_semaphore()
     for r in range(1, n):
@@ -112,70 +128,75 @@
         hid.at[:, pl.ds(pl.multiple_of(me * kblk, 128), kblk)], own, osem
     )
     load_own.start()
-    load_hi = pltpu.make_async_copy(whi_h, whi, wsem.at[0])
-    load_lo = pltpu.make_async_copy(wlo_h, wlo, wsem.at[1])
-    load_hi.start()
-    load_lo.start()
+    depth = stage.shape[1]
+    loads = kblk // depth
+
+    def load_weight(i):
+        slot = lax.rem(i, 2)
+        return pltpu.make_async_copy(
+            weight.at[pl.ds(pl.multiple_of(i * depth, depth), depth)], stage.at[slot], wsem.at[slot]
+        )
+
+    load_weight(0).start()
     pl.semaphore_wait(barrier, n)
 
     def rows_of(which, q):
         return pl.ds(pl.multiple_of(which * half + q * chunk, chunk), chunk)
 
-    def hidden_copy(q, r):
-        p = lax.rem(me + r, n)
+    def hidden_copy(q, m):
+        p = peer(m)
         return pltpu.make_async_remote_copy(
             src_ref=hid.at[rows_of(core, q), pl.ds(pl.multiple_of(p * kblk, 128), kblk)],
-            dst_ref=got.at[n - r - 1, rows_of(core, q)],
-            send_sem=hsend.at[q, r - 1],
-            recv_sem=hrecv.at[q, n - r - 1],
+            dst_ref=got.at[m - 1, rows_of(core, q)],
+            send_sem=hsend.at[q, m - 1],
+            recv_sem=hrecv.at[q, m - 1],
             device_id={"seq": p},
             device_id_type=MESH,
         )
 
-    def hidden_arrival(q, slot):
-        return pltpu.make_async_remote_copy(
-            src_ref=got.at[slot, rows_of(core, q)],
-            dst_ref=got.at[slot, rows_of(core, q)],
-            send_sem=hsend.at[q, slot],
-            recv_sem=hrecv.at[q, slot],
-            device_id={"seq": lax.rem(me + slot + 1, n)},
-            device_id_type=MESH,
-        )
-
-    def forward_copy(q, slot, which):
-        return pltpu.make_async_remote_copy(
-            src_ref=got.at[slot, rows_of(which, q)],
-            dst_ref=got.at[slot, rows_of(which, q)],
-            send_sem=fsend.at[q, slot],
-            recv_sem=frsem.at[q, slot],
+    def hidden_arrival(q, m):
+        return pltpu.make_async_remote_copy(
+            src_ref=got.at[m - 1, rows_of(core, q)],
+            dst_ref=got.at[m - 1, rows_of(core, q)],
+            send_sem=hsend.at[q, m - 1],
+            recv_sem=hrecv.at[q, m - 1],
+            device_id={"seq": peer(m)},
+            device_id_type=MESH,
+        )
+
+    def forward_copy(q, m, which):
+        return pltpu.make_async_remote_copy(
+            src_ref=got.at[m - 1, rows_of(which, q)],
+            dst_ref=got.at[m - 1, rows_of(which, q)],
+            send_sem=fsend.at[q, m - 1],
+            recv_sem=frsem.at[q, m - 1],
             device_id={"head": 1 - core},
             device_id_type=MESH,
         )
 
+    def via_copy(which, q):
+        return pltpu.make_async_remote_copy(
+            src_ref=part.at[2, rows_of(which, q)],
+            dst_ref=sums.at[2, rows_of(which, q)],
+            send_sem=psend.at[2, which, q],
+            recv_sem=precv.at[2, which, q],
+            device_id={"seq": which * across[1] + (1 - which) * across[2]},
+            device_id_type=MESH,
+        )
+
     def part_copy(slot, which, q):
-        r = slot + 1
         return pltpu.make_async_remote_copy(
             src_ref=part.at[slot, rows_of(which, q)],
-            dst_ref=sums.at[n - r - 1, rows_of(which, q)],
-            send_sem=psend.at[slot, which, q],
-            recv_sem=precv.at[n - r - 1, which, q],
-            device_id={"seq": lax.rem(me + r, n)},
-            device_id_type=MESH,
-        )
-
-    def part_arrival(slot, which, q):
-        return pltpu.make_async_remote_copy(
-            src_ref=sums.at[slot, rows_of(which, q)],
             dst_ref=sums.at[slot, rows_of(which, q)],
             send_sem=psend.at[slot, which, q],
             recv_sem=precv.at[slot, which, q],
-            device_id={"seq": lax.rem(me + slot + 1, n)},
+            device_id={"seq": (1 - slot) * across[1] + slot * across[2]},
             device_id_type=MESH,
         )
 
     for q in range(pieces):
-        for r in range(1, n):
-            hidden_copy(q, r).start()
+        for m in (3, 1, 2):
+            hidden_copy(q, m).start()
 
     def project(src, dst, rows):
         hi, lo = split(src[rows])
@@ -188,9 +209,21 @@
 
         lax.fori_loop(0, cols // 256, tile, 0)
 
+    def split_weight(i, carry):
+        @pl.when(i + 1 < loads)
+        def _():
+            load_weight(i + 1).start()
+
+        load_weight(i).wait()
+        rows = pl.ds(pl.multiple_of(i * depth, depth), depth)
+        for h in range(heads):
+            hi, lo = split(stage[lax.rem(i, 2), :, h, :])
+            whi[rows, h * 256 : (h + 1) * 256] = hi
+            wlo[rows, h * 256 : (h + 1) * 256] = lo
+        return carry
+
+    lax.fori_loop(0, loads, split_weight, 0)
     load_own.wait()
-    load_hi.wait()
-    load_lo.wait()
 
     def own_step(i, carry):
         project(own, res, pl.ds(pl.multiple_of(i * chunk, chunk), chunk))
@@ -198,27 +231,41 @@
 
     lax.fori_loop(0, tok // chunk, own_step, 0)
 
+    def pass_on(i):
+        q = i // 2
+        which = lax.rem(core + i, 2)
+        rows = rows_of(which, q)
+        via_copy(which, q).wait_recv()
+        part[which, rows] = part[which, rows] + sums[2, rows]
+        part_copy(which, which, q).start()
+
     def step(i, carry):
-        q = i // (n - 1)
-        slot = lax.rem(i, n - 1)
-        hidden_arrival(q, slot).wait_recv()
-        forward_copy(q, slot, core).start()
-
-        def side(j, carry):
-            which = lax.rem(core + j, 2)
-
-            @pl.when(j == 1)
+        q = i // 2
+        which = lax.rem(core + i, 2)
+        for m in (3, 1, 2):
+
+            @pl.when(lax.rem(i, 2) == 0)
             def _():
-                forward_copy(q, slot, which).wait_recv()
-
-            project(got.at[slot], part.at[slot], rows_of(which, q))
-            part_copy(slot, which, q).start()
-            return carry
-
-        lax.fori_loop(0, 2, side, 0)
+                hidden_arrival(q, m).wait_recv()
+                forward_copy(q, m, core).start()
+
+            @pl.when(lax.rem(i, 2) == 1)
+            def _():
+                forward_copy(q, m, 1 - core).wait_recv()
+
+            project(got.at[m - 1], part.at[m - 1], rows_of(which, q))
+            if m == 3:
+                via_copy(which, q).start()
+        part_copy(1 - which, which, q).start()
+
+        @pl.when(i > 0)
+        def _():
+            pass_on(i - 1)
+
         return carry
 
-    lax.fori_loop(0, pieces * (n - 1), step, 0)
+    lax.fori_loop(0, 2 * pieces, step, 0)
+    pass_on(2 * pieces - 1)
 
     group = tok // groups
     per = chunk // group
@@ -226,13 +273,13 @@
     def residual(i, carry):
         which = i // pieces
         q = lax.rem(i, pieces)
-        for slot in range(n - 1):
-            part_arrival(slot, which, q).wait_recv()
+        for slot in range(2):
+            part_copy(slot, which, q).wait_recv()
         for g in range(per):
             at = i * per + g
             rows = pl.ds(pl.multiple_of(at * group, group), group)
             kv = res[rows]
-            for slot in range(n - 1):
+            for slot in range(2):
                 kv = kv + sums[slot, rows]
             kv = kv * scale[rows]
             spacing = jnp.max(jnp.abs(kv), axis=0, keepdims=True) / 7.0 + 1e-06
@@ -253,21 +300,20 @@
 
     lax.fori_loop(0, heads, square, 0)
 
-    def gram_copy(r):
-        p = peer(r)
-        return pltpu.make_async_remote_copy(
-            src_ref=gsend.at[p],
-            dst_ref=grecv.at[n - r - 1],
-            send_sem=gs.at[r - 1],
-            recv_sem=gr.at[n - r - 1],
-            device_id={"seq": p},
-            device_id_type=MESH,
-        )
-
-    for r in range(1, n):
-        gram_copy(r).start()
-    for r in range(1, n):
-        gram_copy(r).wait_recv()
+    def gram_copy(m):
+        return pltpu.make_async_remote_copy(
+            src_ref=gsend.at[peer(m)],
+            dst_ref=grecv.at[m - 1],
+            send_sem=gs.at[m - 1],
+            recv_sem=gr.at[m - 1],
+            device_id={"seq": peer(m)},
+            device_id_type=MESH,
+        )
+
+    for m in (3, 1, 2):
+        gram_copy(m).start()
+    for m in range(1, n):
+        gram_copy(m).wait_recv()
 
     total = [gsend[me, e] for e in range(2)]
     for slot in range(n - 1):
@@ -286,18 +332,18 @@
         factors[0, e * rank : (e + 1) * rank] = sketch[e] * root
     factors[1] = jnp.concatenate(coefficient, axis=0).T * (1.0 / root)
 
-    def factor_copy(r):
+    def factor_copy(m):
         return pltpu.make_async_remote_copy(
             src_ref=factors,
-            dst_ref=frecv.at[n - r - 1],
-            send_sem=ms.at[r - 1],
-            recv_sem=mr.at[n - r - 1],
-            device_id={"seq": peer(r)},
-            device_id_type=MESH,
-        )
-
-    for r in range(1, n):
-        factor_copy(r).start()
+            dst_ref=frecv.at[m - 1],
+            send_sem=ms.at[m - 1],
+            recv_sem=mr.at[m - 1],
+            device_id={"seq": peer(m)},
+            device_id_type=MESH,
+        )
+
+    for m in (3, 1, 2):
+        factor_copy(m).start()
 
     def finish(h, matrix, coefficient_rows):
         zero = jnp.zeros((rank, 128), jnp.float32)
@@ -315,20 +361,21 @@
         right[h] = coefficient_rows
 
     finish(me, factors[0], factors[1])
-    for r in range(1, n):
-        slot = r - 1
-        factor_copy(n - r).wait_recv()
-        finish(peer(r), frecv[slot, 0], frecv[slot, 1])
+    for m in range(1, n):
+        factor_copy(m).wait_recv()
+        finish(peer(m), frecv[m - 1, 0], frecv[m - 1, 1])
 
     for q in range(pieces):
-        for r in range(1, n):
-            hidden_copy(q, r).wait_send()
-            forward_copy(q, r - 1, core).wait_send()
-            for which in range(2):
-                part_copy(r - 1, which, q).wait_send()
-    for r in range(1, n):
-        gram_copy(r).wait_send()
-        factor_copy(r).wait_send()
+        for m in range(1, n):
+            hidden_copy(q, m).wait_send()
+            forward_copy(q, m, core).wait_send()
+        for which in range(2):
+            via_copy(which, q).wait_send()
+            for slot in range(2):
+                part_copy(slot, which, q).wait_send()
+    for m in range(1, n):
+        gram_copy(m).wait_send()
+        factor_copy(m).wait_send()
 
 
 def fast_shards(n, hidden, row_scale, key_value_weight, outlier, sketch_sign_flags):
@@ -336,10 +383,6 @@
     kblk, heads, per_head = key_value_weight.shape
     cols = heads * per_head
     groups = outlier.shape[0]
-    flat = key_value_weight.reshape(kblk, cols)
-    top = lax.reduce_precision(flat, exponent_bits=8, mantissa_bits=7)
-    whi = top.astype(jnp.bfloat16)
-    wlo = (flat - top).astype(jnp.bfloat16)
     retain = jnp.repeat((1 - outlier).astype(jnp.float32), per_head, axis=1)
     signs = (2 * sketch_sign_flags - 1).astype(jnp.float32).transpose(0, 1, 3, 2)
     f32 = jnp.float32
@@ -352,11 +395,12 @@
             jax.ShapeDtypeStruct((heads, tok, 128), jnp.bfloat16),
             jax.ShapeDtypeStruct((heads, 128, 128), f32),
         ),
-        in_specs=[any_spec, any_spec, any_spec, vmem, vmem, vmem],
+        in_specs=[any_spec, any_spec, vmem, vmem, vmem],
         out_specs=(vmem, vmem),
         scratch_shapes=[
             pltpu.VMEM((kblk, cols), jnp.bfloat16),
             pltpu.VMEM((kblk, cols), jnp.bfloat16),
+            pltpu.VMEM((2, math.gcd(kblk, 256), heads, per_head), f32),
             pltpu.VMEM((tok, kblk), f32),
             pltpu.VMEM((n - 1, tok, kblk), f32),
             pltpu.VMEM((n - 1, tok, cols), f32),
@@ -385,7 +429,7 @@
         cost_estimate=pl.CostEstimate(
             flops=6 * n * tok * kblk * cols, bytes_accessed=4 * n * tok * kblk, transcendentals=0
         ),
-    )(hidden, whi, wlo, row_scale[:, None], retain, signs)
+    )(hidden, key_value_weight, row_scale[:, None], retain, signs)
     return left, right
 
 

time: 241 us -> 201 us (0.83)
  Pallas kernels: 223 us -> 192 us
  local copies, waits for them, and re-layouts: 10.6 us -> 5.76 us
  other arithmetic: 5.84 us -> 2.37 us
    pallas_call x1, Pallas kernels: 223 us -> 192 us  [fast_shards(): pl.pallas_call(functools.partial(kernel, n, groups, math.sqrt(tok * n)),...]
    unnamed x9 -> x2, local copies, waits for them, and re-layouts: 9.02 us -> 3.54 us
    convert_element_type x1 -> x0, other arithmetic: 5.11 us -> none  [fast_shards(): wlo = (flat - top).astype(jnp.bfloat16)]
where the time goes in v2:
time: 201 us
  Pallas kernels  192 us (96%)
  local copies, waits for them, and re-layouts  5.76 us (3%)
  other arithmetic  2.37 us (1%)
    pallas_call x1, Pallas kernels, fast_shards(): pl.pallas_call(functools.partial(kernel, n, groups, math.sqrt(tok * n)),...  192 us

profile of v2, /device:TPU:0, one launch (start us, length us, event | category | flops | bytes accessed | tf_op | source)
XLA Modules:
  0.0 200.5 jit_solution(2440156804309668167)
XLA Ops:
  0.6 0.7 subtract_convert_fusion
  1.3 0.7 broadcast_in_dim.7
  2.0 1.5 copy.7.scale
  3.5 1.7 convert_bitcast_fusion.signs
  5.2 191.7 %shard_map.68 = (bf16[4,512,128]{2,1,0:T(8,128)(2,1)}, f32[4,128,128]{2,1,0:T(8,128)}) custom-call(f32[512,8192]{1,0:T(8,128)} %hid.1, f32[2048,4,256]{2,1,0:T(4,128)} %weight.1, f32[512,1]{1,0:T(8,128)} %copy.7.scale, f32[8,1024]{1,0:T(8,128)} %bitcast.4, f32[4,2,64,128]{3,2,1,0:T(8,128)} %convert_bitcast_fusion.signs), custom_call_target="tpu_custom_call" | custom-call | flops 25769803776 | bytes 16777216 | tf_op jit(solution)/shard_map/pallas_call | solution.py:392
  197.0 1.9 copy.10
  198.8 1.7 copy.11

commit v3 on v2

--- a/solution.py
+++ b/solution.py
@@ -11,6 +11,8 @@
 
 ITERS = 2
 BLOCK = 4
+PIECES = 2
+AHEAD = 3
 MESH = pl.DeviceIdType.MESH
 HIGHEST = lax.Precision.HIGHEST
 
@@ -101,192 +103,247 @@
 
 
 def kernel(
-    n, groups, root, hid, weight, scale, retain, signs, left, right,
+    n, groups, root, hid, weight, scale, retain, signs, left, right, landed,
     whi, wlo, stage, own, got, part, sums, res, gsend, grecv, factors, frecv,
-    wsem, osem, hsend, hrecv, fsend, frsem, psend, precv, gs, gr, ms, mr,
+    lsem, osem, ysend, yrecv, zsend, zrecv, hsend, hrecv, fsend, frsem, psend, precv,
+    gs, gr, ms, mr,
 ):
     me = lax.axis_index("seq")
     core = lax.axis_index("head")
-    tok, kblk = own.shape
+    batch = lax.axis_index("batch")
+    kblk = weight.shape[0]
+    tok = own.shape[0]
     cols = whi.shape[1]
     half = tok // 2
-    pieces = 2
-    chunk = half // pieces
+    chunk = half // PIECES
     heads = cols // 256
-
     across = {1: me + 1 - 2 * lax.rem(me, 2), 2: lax.rem(me + 2, n), 3: n - 1 - me}
+    parity = lax.rem(batch, 2)
+    twin = batch + 1 - 2 * parity
 
     def peer(m):
         return across[m]
 
     barrier = pltpu.get_barrier_semaphore()
-    for r in range(1, n):
-        pl.semaphore_signal(barrier, inc=1, device_id={"seq": peer(r)}, device_id_type=MESH)
+    for m in range(1, n):
+        pl.semaphore_signal(barrier, inc=1, device_id={"seq": peer(m)}, device_id_type=MESH)
     pl.semaphore_signal(barrier, inc=1, device_id={"head": 1 - core}, device_id_type=MESH)
-
-    load_own = pltpu.make_async_copy(
-        hid.at[:, pl.ds(pl.multiple_of(me * kblk, 128), kblk)], own, osem
-    )
-    load_own.start()
+    pl.semaphore_signal(barrier, inc=1, device_id={"batch": twin}, device_id_type=MESH)
+
+    def columns_of(member):
+        return pl.ds(pl.multiple_of(member * kblk, 128), kblk)
+
+    load_own = [
+        pltpu.make_async_copy(
+            hid.at[:, columns_of(p)], own.at[:, pl.ds(b * kblk, kblk)], osem.at[b]
+        )
+        for b, p in enumerate((me, across[2]))
+    ]
+    for copy in load_own:
+        copy.start()
     depth = stage.shape[1]
     loads = kblk // depth
 
-    def load_weight(i):
-        slot = lax.rem(i, 2)
+    def load_weight(source, i, slot):
         return pltpu.make_async_copy(
-            weight.at[pl.ds(pl.multiple_of(i * depth, depth), depth)], stage.at[slot], wsem.at[slot]
-        )
-
-    load_weight(0).start()
-    pl.semaphore_wait(barrier, n)
+            source.at[pl.ds(pl.multiple_of(i * depth, depth), depth)], stage.at[slot], lsem.at[slot]
+        )
+
+    def split_stage(slot, at):
+        rows = pl.ds(pl.multiple_of(at, depth), depth)
+        for h in range(heads):
+            hi, lo = split(stage[slot, :, h, :])
+            whi[rows, h * 256 : (h + 1) * 256] = hi
+            wlo[rows, h * 256 : (h + 1) * 256] = lo
+
+    load_weight(weight, 0, 0).start()
+    pl.semaphore_wait(barrier, n + 1)
 
     def rows_of(which, q):
         return pl.ds(pl.multiple_of(which * half + q * chunk, chunk), chunk)
 
-    def hidden_copy(q, m):
-        p = peer(m)
-        return pltpu.make_async_remote_copy(
-            src_ref=hid.at[rows_of(core, q), pl.ds(pl.multiple_of(p * kblk, 128), kblk)],
-            dst_ref=got.at[m - 1, rows_of(core, q)],
-            send_sem=hsend.at[q, m - 1],
-            recv_sem=hrecv.at[q, m - 1],
-            device_id={"seq": p},
-            device_id_type=MESH,
-        )
-
-    def hidden_arrival(q, m):
-        return pltpu.make_async_remote_copy(
-            src_ref=got.at[m - 1, rows_of(core, q)],
-            dst_ref=got.at[m - 1, rows_of(core, q)],
-            send_sem=hsend.at[q, m - 1],
-            recv_sem=hrecv.at[q, m - 1],
-            device_id={"seq": peer(m)},
-            device_id_type=MESH,
-        )
-
-    def forward_copy(q, m, which):
-        return pltpu.make_async_remote_copy(
-            src_ref=got.at[m - 1, rows_of(which, q)],
-            dst_ref=got.at[m - 1, rows_of(which, q)],
-            send_sem=fsend.at[q, m - 1],
-            recv_sem=frsem.at[q, m - 1],
+    share = loads // 2
+
+    def weight_rows(which, i):
+        return pl.ds(pl.multiple_of((which * share + i) * depth, depth), depth)
+
+    def weight_copy(i):
+        return pltpu.make_async_remote_copy(
+            src_ref=weight.at[weight_rows(parity, i)],
+            dst_ref=landed.at[weight_rows(parity, i)],
+            send_sem=ysend.at[i],
+            recv_sem=yrecv.at[i],
+            device_id={"seq": across[2]},
+            device_id_type=MESH,
+        )
+
+    def twin_copy(i, which):
+        return pltpu.make_async_remote_copy(
+            src_ref=landed.at[weight_rows(which, i)],
+            dst_ref=landed.at[weight_rows(which, i)],
+            send_sem=zsend.at[i],
+            recv_sem=zrecv.at[i],
+            device_id={"batch": twin},
+            device_id_type=MESH,
+        )
+
+    def hidden_copy(q, b):
+        return pltpu.make_async_remote_copy(
+            src_ref=hid.at[rows_of(core, q), columns_of((1 - b) * across[1] + b * across[3])],
+            dst_ref=got.at[rows_of(core, q), columns_of(b)],
+            send_sem=hsend.at[q, b],
+            recv_sem=hrecv.at[q, b],
+            device_id={"seq": across[1]},
+            device_id_type=MESH,
+        )
+
+    def forward_copy(q, b, which):
+        return pltpu.make_async_remote_copy(
+            src_ref=got.at[rows_of(which, q), columns_of(b)],
+            dst_ref=got.at[rows_of(which, q), columns_of(b)],
+            send_sem=fsend.at[q, b],
+            recv_sem=frsem.at[q, b],
             device_id={"head": 1 - core},
             device_id_type=MESH,
         )
 
-    def via_copy(which, q):
-        return pltpu.make_async_remote_copy(
-            src_ref=part.at[2, rows_of(which, q)],
-            dst_ref=sums.at[2, rows_of(which, q)],
-            send_sem=psend.at[2, which, q],
-            recv_sem=precv.at[2, which, q],
-            device_id={"seq": which * across[1] + (1 - which) * across[2]},
-            device_id_type=MESH,
-        )
-
-    def part_copy(slot, which, q):
-        return pltpu.make_async_remote_copy(
-            src_ref=part.at[slot, rows_of(which, q)],
-            dst_ref=sums.at[slot, rows_of(which, q)],
-            send_sem=psend.at[slot, which, q],
-            recv_sem=precv.at[slot, which, q],
-            device_id={"seq": (1 - slot) * across[1] + slot * across[2]},
-            device_id_type=MESH,
-        )
-
-    for q in range(pieces):
-        for m in (3, 1, 2):
-            hidden_copy(q, m).start()
-
-    def project(src, dst, rows):
-        hi, lo = split(src[rows])
+    def part_copy(which, q):
+        return pltpu.make_async_remote_copy(
+            src_ref=part.at[rows_of(which, q)],
+            dst_ref=sums.at[rows_of(which, q)],
+            send_sem=psend.at[which, q],
+            recv_sem=precv.at[which, q],
+            device_id={"seq": across[1]},
+            device_id_type=MESH,
+        )
+
+    def project(src, dst, rows, b, add):
+        hi, lo = split(src[rows, b * kblk : (b + 1) * kblk])
+        depths = slice(b * kblk, (b + 1) * kblk)
 
         def tile(t, carry):
             c = pl.ds(pl.multiple_of(t * 256, 256), 256)
-            w = whi[:, c]
-            dst[rows, c] = dot(hi, w) + dot(lo, w) + dot(hi, wlo[:, c])
+            w = whi[depths, c]
+            value = dot(hi, w) + dot(lo, w) + dot(hi, wlo[depths, c])
+            dst[rows, c] = dst[rows, c] + value if add else value
             return carry
 
         lax.fori_loop(0, cols // 256, tile, 0)
 
-    def split_weight(i, carry):
+    hidden_order = [(q, b) for q in range(PIECES) for b in range(2)]
+    for i in range(AHEAD):
+        weight_copy(i).start()
+    for q, b in hidden_order[:2]:
+        hidden_copy(q, b).start()
+
+    def split_own(i, carry):
+        slot = lax.rem(i, 2)
+
         @pl.when(i + 1 < loads)
         def _():
-            load_weight(i + 1).start()
-
-        load_weight(i).wait()
-        rows = pl.ds(pl.multiple_of(i * depth, depth), depth)
-        for h in range(heads):
-            hi, lo = split(stage[lax.rem(i, 2), :, h, :])
-            whi[rows, h * 256 : (h + 1) * 256] = hi
-            wlo[rows, h * 256 : (h + 1) * 256] = lo
-        return carry
-
-    lax.fori_loop(0, loads, split_weight, 0)
-    load_own.wait()
-
-    def own_step(i, carry):
-        project(own, res, pl.ds(pl.multiple_of(i * chunk, chunk), chunk))
-        return carry
-
-    lax.fori_loop(0, tok // chunk, own_step, 0)
-
-    def pass_on(i):
+            load_weight(weight, i + 1, 1 - slot).start()
+
+        load_weight(weight, i, slot).wait()
+        split_stage(slot, i * depth)
+        return carry
+
+    lax.fori_loop(0, loads, split_own, 0)
+    for copy in load_own:
+        copy.wait()
+
+    def own_first(i, carry):
+        project(own, res, pl.ds(pl.multiple_of(i * chunk, chunk), chunk), 0, False)
+        return carry
+
+    lax.fori_loop(0, 2 * PIECES, own_first, 0)
+
+    every = share // len(hidden_order)
+
+    def arrive(i, carry):
+        weight_copy(i).wait_recv()
+        twin_copy(i, parity).start()
+
+        @pl.when(i + AHEAD < share)
+        def _():
+            weight_copy(i + AHEAD).start()
+
+        direct = load_weight(landed, parity * share + i, 0)
+        direct.start()
+
+        @pl.when(lax.rem(i, every) == every - 1)
+        def _():
+            at = i // every
+            hidden_copy(at // 2, lax.rem(at, 2)).wait_recv()
+            forward_copy(at // 2, lax.rem(at, 2), core).start()
+
+            @pl.when(at + 2 < len(hidden_order))
+            def _():
+                hidden_copy(at // 2 + 1, lax.rem(at, 2)).start()
+
+        def passed():
+            return load_weight(landed, (1 - parity) * share + i - 1, 1)
+
+        @pl.when(i > 0)
+        def _():
+            twin_copy(i - 1, 1 - parity).wait_recv()
+            passed().start()
+
+        direct.wait()
+        split_stage(0, kblk + (parity * share + i) * depth)
+
+        @pl.when(i > 0)
+        def _():
+            passed().wait()
+            split_stage(1, kblk + ((1 - parity) * share + i - 1) * depth)
+
+        return carry
+
+    lax.fori_loop(0, share, arrive, 0)
+    twin_copy(share - 1, 1 - parity).wait_recv()
+    passed = load_weight(landed, (1 - parity) * share + share - 1, 1)
+    passed.start()
+    passed.wait()
+    split_stage(1, kblk + ((1 - parity) * share + share - 1) * depth)
+
+    def neighbour(i, carry):
         q = i // 2
         which = lax.rem(core + i, 2)
+
+        @pl.when(lax.rem(i, 2) == 1)
+        def _():
+            for b in range(2):
+                forward_copy(q, b, which).wait_recv()
+
         rows = rows_of(which, q)
-        via_copy(which, q).wait_recv()
-        part[which, rows] = part[which, rows] + sums[2, rows]
-        part_copy(which, which, q).start()
-
-    def step(i, carry):
+        project(got, part, rows, 0, False)
+        project(got, part, rows, 1, True)
+        part_copy(which, q).start()
+        return carry
+
+    lax.fori_loop(0, 2 * PIECES, neighbour, 0)
+
+    def own_step(i, carry):
+        project(own, res, pl.ds(pl.multiple_of(i * chunk, chunk), chunk), 1, True)
+        return carry
+
+    lax.fori_loop(0, 2 * PIECES, own_step, 0)
+
+    group = tok // groups
+    per = chunk // group
+
+    def residual(i, carry):
         q = i // 2
         which = lax.rem(core + i, 2)
-        for m in (3, 1, 2):
-
-            @pl.when(lax.rem(i, 2) == 0)
-            def _():
-                hidden_arrival(q, m).wait_recv()
-                forward_copy(q, m, core).start()
-
-            @pl.when(lax.rem(i, 2) == 1)
-            def _():
-                forward_copy(q, m, 1 - core).wait_recv()
-
-            project(got.at[m - 1], part.at[m - 1], rows_of(which, q))
-            if m == 3:
-                via_copy(which, q).start()
-        part_copy(1 - which, which, q).start()
-
-        @pl.when(i > 0)
-        def _():
-            pass_on(i - 1)
-
-        return carry
-
-    lax.fori_loop(0, 2 * pieces, step, 0)
-    pass_on(2 * pieces - 1)
-
-    group = tok // groups
-    per = chunk // group
-
-    def residual(i, carry):
-        which = i // pieces
-        q = lax.rem(i, pieces)
-        for slot in range(2):
-            part_copy(slot, which, q).wait_recv()
+        part_copy(which, q).wait_recv()
         for g in range(per):
-            at = i * per + g
+            at = (which * PIECES + q) * per + g
             rows = pl.ds(pl.multiple_of(at * group, group), group)
-            kv = res[rows]
-            for slot in range(2):
-                kv = kv + sums[slot, rows]
-            kv = kv * scale[rows]
+            kv = (res[rows] + sums[rows]) * scale[rows]
             spacing = jnp.max(jnp.abs(kv), axis=0, keepdims=True) / 7.0 + 1e-06
             res[rows] = retain[pl.ds(at, 1)] * sine_of_cycles(kv * (1.0 / spacing))
         return carry
 
-    lax.fori_loop(0, 2 * pieces, residual, 0)
+    lax.fori_loop(0, 2 * PIECES, residual, 0)
 
     def square(h, carry):
         for e in range(2):
@@ -365,14 +422,14 @@
         factor_copy(m).wait_recv()
         finish(peer(m), frecv[m - 1, 0], frecv[m - 1, 1])
 
-    for q in range(pieces):
-        for m in range(1, n):
-            hidden_copy(q, m).wait_send()
-            forward_copy(q, m, core).wait_send()
-        for which in range(2):
-            via_copy(which, q).wait_send()
-            for slot in range(2):
-                part_copy(slot, which, q).wait_send()
+    for i in range(share):
+        weight_copy(i).wait_send()
+        twin_copy(i, parity).wait_send()
+    for q in range(PIECES):
+        for b in range(2):
+            hidden_copy(q, b).wait_send()
+            forward_copy(q, b, core).wait_send()
+            part_copy(b, q).wait_send()
     for m in range(1, n):
         gram_copy(m).wait_send()
         factor_copy(m).wait_send()
@@ -389,35 +446,41 @@
     any_spec = pl.BlockSpec(memory_space=pl.ANY)
     vmem = pl.BlockSpec(memory_space=pltpu.VMEM)
     dma = pltpu.SemaphoreType.DMA
-    left, right = pl.pallas_call(
+    depth = kblk // 16
+    left, right, _ = pl.pallas_call(
         functools.partial(kernel, n, groups, math.sqrt(tok * n)),
         out_shape=(
             jax.ShapeDtypeStruct((heads, tok, 128), jnp.bfloat16),
             jax.ShapeDtypeStruct((heads, 128, 128), f32),
+            jax.ShapeDtypeStruct((kblk, heads, per_head), f32),
         ),
         in_specs=[any_spec, any_spec, vmem, vmem, vmem],
-        out_specs=(vmem, vmem),
+        out_specs=(vmem, vmem, any_spec),
         scratch_shapes=[
-            pltpu.VMEM((kblk, cols), jnp.bfloat16),
-            pltpu.VMEM((kblk, cols), jnp.bfloat16),
-            pltpu.VMEM((2, math.gcd(kblk, 256), heads, per_head), f32),
-            pltpu.VMEM((tok, kblk), f32),
-            pltpu.VMEM((n - 1, tok, kblk), f32),
-            pltpu.VMEM((n - 1, tok, cols), f32),
-            pltpu.VMEM((n - 1, tok, cols), f32),
+            pltpu.VMEM((2 * kblk, cols), jnp.bfloat16),
+            pltpu.VMEM((2 * kblk, cols), jnp.bfloat16),
+            pltpu.VMEM((2, depth, heads, per_head), f32),
+            pltpu.VMEM((tok, 2 * kblk), f32),
+            pltpu.VMEM((tok, 2 * kblk), f32),
+            pltpu.VMEM((tok, cols), f32),
+            pltpu.VMEM((tok, cols), f32),
             pltpu.VMEM((tok, cols), f32),
             pltpu.VMEM((heads, 2, 128, 128), f32),
             pltpu.VMEM((n - 1, 2, 128, 128), f32),
             pltpu.VMEM((2, 128, 128), f32),
             pltpu.VMEM((n - 1, 2, 128, 128), f32),
             dma((2,)),
-            dma,
-            dma((2, n - 1)),
-            dma((2, n - 1)),
-            dma((2, n - 1)),
-            dma((2, n - 1)),
-            dma((n - 1, 2, 2)),
-            dma((n - 1, 2, 2)),
+            dma((2,)),
+            dma((8,)),
+            dma((8,)),
+            dma((8,)),
+            dma((8,)),
+            dma((PIECES, 2)),
+            dma((PIECES, 2)),
+            dma((PIECES, 2)),
+            dma((PIECES, 2)),
+            dma((2, PIECES)),
+            dma((2, PIECES)),
             dma((n - 1,)),
             dma((n - 1,)),
             dma((n - 1,)),
@@ -487,7 +550,8 @@
     def run(hidden, row_scale, key_value_weight, outlier, sketch_sign_flags):
         members = mesh.shape["seq"]
         heads = key_value_weight.shape[1] // mesh.shape["head"]
-        fits = members == 4 and heads == members and mesh.shape["head"] == 2
+        fits = members == 4 and heads == members
+        fits = fits and mesh.shape["head"] == 2 and mesh.shape["batch"] % 2 == 0
         chosen = functools.partial(fast_shards, members) if fits else shards
         return mapped(chosen)(hidden, row_scale, key_value_weight, outlier, sketch_sign_flags)
 

time: 201 us -> 225 us (1.12)
  Pallas kernels: 192 us -> 215 us
    pallas_call x1, Pallas kernels: 192 us -> 215 us  [fast_shards(): pl.pallas_call(functools.partial(kernel, n, groups, math.sqrt(tok * n)),...]
where the time goes in v3:
time: 225 us; the launch traced here: 224 us
  Pallas kernels  215 us (96%)
  local copies, waits for them, and re-layouts  5.75 us (3%)
  other arithmetic  2.37 us (1%)
    pallas_call x1, Pallas kernels, fast_shards(): pl.pallas_call(functools.partial(kernel, n, groups, math.sqrt(tok * n)),...  215 us

profile of v3, /device:TPU:0, one launch (start us, length us, event | category | flops | bytes accessed | tf_op | source)
XLA Modules:
  0.0 224.2 jit_solution(6988689214007303370)
XLA Ops:
  0.6 0.7 subtract_convert_fusion
  1.3 0.7 broadcast_in_dim.7
  2.0 1.5 copy.7.scale
  3.5 1.7 convert_bitcast_fusion.signs
  5.2 215.4 %shard_map.68 = (bf16[4,512,128]{2,1,0:T(8,128)(2,1)}, f32[4,128,128]{2,1,0:T(8,128)}, f32[2048,4,256]{2,1,0:T(4,128)}) custom-call(f32[512,8192]{1,0:T(8,128)} %hid.1, f32[2048,4,256]{2,1,0:T(4,128)} %weight.1, f32[512,1]{1,0:T(8,128)} %copy.7.scale, f32[8,1024]{1,0:T(8,128)} %bitcast.4, f32[4,2,64,128]{3,2,1,0:T(8,128)} %convert_bitcast_fusion.signs), custom_call_target="tpu_custom_call" | custom-call | flops 25769803776 | bytes 16777216 | tf_op jit(solution)/shard_map/pallas_call | solution.py:450
  220.7 1.9 copy.10
  222.5 1.7 copy.11

commit v4 on v3

--- a/solution.py
+++ b/solution.py
@@ -12,7 +12,7 @@
 ITERS = 2
 BLOCK = 4
 PIECES = 2
-AHEAD = 3
+AHEAD = 4
 MESH = pl.DeviceIdType.MESH
 HIGHEST = lax.Precision.HIGHEST
 
@@ -233,7 +233,7 @@
     hidden_order = [(q, b) for q in range(PIECES) for b in range(2)]
     for i in range(AHEAD):
         weight_copy(i).start()
-    for q, b in hidden_order[:2]:
+    for q, b in hidden_order:
         hidden_copy(q, b).start()
 
     def split_own(i, carry):
@@ -257,7 +257,6 @@
 
     lax.fori_loop(0, 2 * PIECES, own_first, 0)
 
-    every = share // len(hidden_order)
 
     def arrive(i, carry):
         weight_copy(i).wait_recv()
@@ -269,16 +268,6 @@
 
         direct = load_weight(landed, parity * share + i, 0)
         direct.start()
-
-        @pl.when(lax.rem(i, every) == every - 1)
-        def _():
-            at = i // every
-            hidden_copy(at // 2, lax.rem(at, 2)).wait_recv()
-            forward_copy(at // 2, lax.rem(at, 2), core).start()
-
-            @pl.when(at + 2 < len(hidden_order))
-            def _():
-                hidden_copy(at // 2 + 1, lax.rem(at, 2)).start()
 
         def passed():
             return load_weight(landed, (1 - parity) * share + i - 1, 1)
@@ -305,11 +294,17 @@
     passed.wait()
     split_stage(1, kblk + ((1 - parity) * share + share - 1) * depth)
 
+    for q, b in hidden_order:
+        hidden_copy(q, b).wait_recv()
+        forward_copy(q, b, core).start()
+
+    def turn(i):
+        return lax.rem(i, PIECES), lax.rem(core + i // PIECES, 2)
+
     def neighbour(i, carry):
-        q = i // 2
-        which = lax.rem(core + i, 2)
-
-        @pl.when(lax.rem(i, 2) == 1)
+        q, which = turn(i)
+
+        @pl.when(i >= PIECES)
         def _():
             for b in range(2):
                 forward_copy(q, b, which).wait_recv()
@@ -332,8 +327,7 @@
     per = chunk // group
 
     def residual(i, carry):
-        q = i // 2
-        which = lax.rem(core + i, 2)
+        q, which = turn(i)
         part_copy(which, q).wait_recv()
         for g in range(per):
             at = (which * PIECES + q) * per + g
@@ -341,21 +335,22 @@
             kv = (res[rows] + sums[rows]) * scale[rows]
             spacing = jnp.max(jnp.abs(kv), axis=0, keepdims=True) / 7.0 + 1e-06
             res[rows] = retain[pl.ds(at, 1)] * sine_of_cycles(kv * (1.0 / spacing))
-        return carry
-
+        rows = rows_of(which, q)
+
+        def square(h, carry):
+            for e in range(2):
+                hi, lo = split(res[rows, pl.ds(pl.multiple_of(h * 256 + e * 128, 128), 128)])
+                both = jnp.concatenate([hi, lo], axis=1)
+                g = lax.dot_general(
+                    both, both, (((0,), (0,)), ((), ())), preferred_element_type=jnp.float32
+                )
+                gsend[h, e] += g[:128, :128] + (g[:128, 128:] + g[128:, :128])
+            return carry
+
+        return lax.fori_loop(0, heads, square, carry)
+
+    gsend[...] = jnp.zeros_like(gsend)
     lax.fori_loop(0, 2 * PIECES, residual, 0)
-
-    def square(h, carry):
-        for e in range(2):
-            hi, lo = split(res[:, pl.ds(pl.multiple_of(h * 256 + e * 128, 128), 128)])
-            both = jnp.concatenate([hi, lo], axis=1)
-            g = lax.dot_general(
-                both, both, (((0,), (0,)), ((), ())), preferred_element_type=jnp.float32
-            )
-            gsend[h, e] = g[:128, :128] + (g[:128, 128:] + g[128:, :128])
-        return carry
-
-    lax.fori_loop(0, heads, square, 0)
 
     def gram_copy(m):
         return pltpu.make_async_remote_copy(

time: 225 us -> 224 us (level)
  no operation moved by 1% of the time
where the time goes in v4:
time: 224 us
  Pallas kernels  215 us (96%)
  local copies, waits for them, and re-layouts  5.75 us (3%)
  other arithmetic  2.37 us (1%)
    pallas_call x1, Pallas kernels, fast_shards(): pl.pallas_call(functools.partial(kernel, n, groups, math.sqrt(tok * n)),...  215 us

profile of v4, /device:TPU:0, one launch (start us, length us, event | category | flops | bytes accessed | tf_op | source)
XLA Modules:
  0.0 223.8 jit_solution(12208016609356227497)
XLA Ops:
  0.6 0.7 subtract_convert_fusion
  1.3 0.7 broadcast_in_dim.7
  2.0 1.5 copy.7.scale
  3.5 1.7 convert_bitcast_fusion.signs
  5.2 215.1 %shard_map.68 = (bf16[4,512,128]{2,1,0:T(8,128)(2,1)}, f32[4,128,128]{2,1,0:T(8,128)}, f32[2048,4,256]{2,1,0:T(4,128)}) custom-call(f32[512,8192]{1,0:T(8,128)} %hid.1, f32[2048,4,256]{2,1,0:T(4,128)} %weight.1, f32[512,1]{1,0:T(8,128)} %copy.7.scale, f32[8,1024]{1,0:T(8,128)} %bitcast.4, f32[4,2,64,128]{3,2,1,0:T(8,128)} %convert_bitcast_fusion.signs), custom_call_target="tpu_custom_call" | custom-call | flops 25769803776 | bytes 16777216 | tf_op jit(solution)/shard_map/pallas_call | solution.py:445
  220.3 1.9 copy.10
  222.2 1.7 copy.11

commit v5 on v2

--- a/solution.py
+++ b/solution.py
@@ -271,12 +271,12 @@
     per = chunk // group
 
     def residual(i, carry):
-        which = i // pieces
-        q = lax.rem(i, pieces)
+        q = i // 2
+        which = lax.rem(core + i, 2)
         for slot in range(2):
             part_copy(slot, which, q).wait_recv()
         for g in range(per):
-            at = i * per + g
+            at = (which * pieces + q) * per + g
             rows = pl.ds(pl.multiple_of(at * group, group), group)
             kv = res[rows]
             for slot in range(2):
@@ -284,21 +284,22 @@
             kv = kv * scale[rows]
             spacing = jnp.max(jnp.abs(kv), axis=0, keepdims=True) / 7.0 + 1e-06
             res[rows] = retain[pl.ds(at, 1)] * sine_of_cycles(kv * (1.0 / spacing))
-        return carry
-
+        rows = rows_of(which, q)
+
+        def square(h, carry):
+            for e in range(2):
+                hi, lo = split(res[rows, pl.ds(pl.multiple_of(h * 256 + e * 128, 128), 128)])
+                both = jnp.concatenate([hi, lo], axis=1)
+                g = lax.dot_general(
+                    both, both, (((0,), (0,)), ((), ())), preferred_element_type=jnp.float32
+                )
+                gsend[h, e] += g[:128, :128] + (g[:128, 128:] + g[128:, :128])
+            return carry
+
+        return lax.fori_loop(0, heads, square, carry)
+
+    gsend[...] = jnp.zeros_like(gsend)
     lax.fori_loop(0, 2 * pieces, residual, 0)
-
-    def square(h, carry):
-        for e in range(2):
-            hi, lo = split(res[:, pl.ds(pl.multiple_of(h * 256 + e * 128, 128), 128)])
-            both = jnp.concatenate([hi, lo], axis=1)
-            g = lax.dot_general(
-                both, both, (((0,), (0,)), ((), ())), preferred_element_type=jnp.float32
-            )
-            gsend[h, e] = g[:128, :128] + (g[:128, 128:] + g[128:, :128])
-        return carry
-
-    lax.fori_loop(0, heads, square, 0)
 
     def gram_copy(m):
         return pltpu.make_async_remote_copy(

time: 201 us -> 202 us (level)
  no operation moved by 1% of the time
where the time goes in v5:
time: 202 us; the launch traced here: 201 us
  Pallas kernels  193 us (96%)
  local copies, waits for them, and re-layouts  5.76 us (3%)
  other arithmetic  2.37 us (1%)
    pallas_call x1, Pallas kernels, fast_shards(): pl.pallas_call(functools.partial(kernel, n, groups, math.sqrt(tok * n)),...  193 us

profile of v5, /device:TPU:0, one launch (start us, length us, event | category | flops | bytes accessed | tf_op | source)
XLA Modules:
  0.0 201.4 jit_solution(1833014561141792349)
XLA Ops:
  0.6 0.7 subtract_convert_fusion
  1.3 0.7 broadcast_in_dim.7
  2.0 1.5 copy.7.scale
  3.5 1.7 convert_bitcast_fusion.signs
  5.2 192.7 %shard_map.68 = (bf16[4,512,128]{2,1,0:T(8,128)(2,1)}, f32[4,128,128]{2,1,0:T(8,128)}) custom-call(f32[512,8192]{1,0:T(8,128)} %hid.1, f32[2048,4,256]{2,1,0:T(4,128)} %weight.1, f32[512,1]{1,0:T(8,128)} %copy.7.scale, f32[8,1024]{1,0:T(8,128)} %bitcast.4, f32[4,2,64,128]{3,2,1,0:T(8,128)} %convert_bitcast_fusion.signs), custom_call_target="tpu_custom_call" | custom-call | flops 25769803776 | bytes 16777216 | tf_op jit(solution)/shard_map/pallas_call | solution.py:393
  197.9 1.9 copy.10
  199.7 1.7 copy.11

commit v6 on v2

--- a/solution.py
+++ b/solution.py
@@ -10,7 +10,7 @@
 from jax.sharding import PartitionSpec as P
 
 ITERS = 2
-BLOCK = 4
+BLOCK = 8
 MESH = pl.DeviceIdType.MESH
 HIGHEST = lax.Precision.HIGHEST
 

time: 201 us -> 203 us (level)
    pallas_call x1, Pallas kernels: 192 us -> 194 us  [fast_shards(): pl.pallas_call(functools.partial(kernel, n, groups, math.sqrt(tok * n)),...]
where the time goes in v6:
time: 203 us
  Pallas kernels  194 us (96%)
  local copies, waits for them, and re-layouts  5.76 us (3%)
  other arithmetic  2.37 us (1%)
    pallas_call x1, Pallas kernels, fast_shards(): pl.pallas_call(functools.partial(kernel, n, groups, math.sqrt(tok * n)),...  194 us

profile of v6, /device:TPU:0, one launch (start us, length us, event | category | flops | bytes accessed | tf_op | source)
XLA Modules:
  0.0 202.5 jit_solution(8415030831097798137)
XLA Ops:
  0.6 0.7 subtract_convert_fusion
  1.3 0.7 broadcast_in_dim.7
  2.0 1.5 copy.7.scale
  3.5 1.7 convert_bitcast_fusion.signs
  5.2 193.8 %shard_map.68 = (bf16[4,512,128]{2,1,0:T(8,128)(2,1)}, f32[4,128,128]{2,1,0:T(8,128)}) custom-call(f32[512,8192]{1,0:T(8,128)} %hid.1, f32[2048,4,256]{2,1,0:T(4,128)} %weight.1, f32[512,1]{1,0:T(8,128)} %copy.7.scale, f32[8,1024]{1,0:T(8,128)} %bitcast.4, f32[4,2,64,128]{3,2,1,0:T(8,128)} %convert_bitcast_fusion.signs), custom_call_target="tpu_custom_call" | custom-call | flops 25769803776 | bytes 16777216 | tf_op jit(solution)/shard_map/pallas_call | solution.py:392
  199.0 1.9 copy.10
  200.9 1.7 copy.11
